TPU v7x, 512 devices: a whole 4x4x16 slice. The times are simulated.
512 devices in a mesh: replica: 64 (over z, x), tensor: 8 (over y, core).
Axes of the slice: x: 4, y: 4, z: 16, core: 2. Of those that a mesh axis runs over, the one named last changes fastest.
Arguments:
- queries: bfloat16 [2048, 2, 8192], P('replica', None, 'tensor'), may hold values from -8.5 to 8.5, as said below
- fresh_entries: bfloat16 [2048, 2, 2, 1024], P('replica', None, None, 'tensor'), may hold values from -8.5 to 8.5, as said below
- suffix_page_pool: bfloat16 [16384, 16, 2, 1024], P('replica', None, None, 'tensor'), may hold values from -6 to 6
- page_table: int32 [2048, 8], P('replica'), may hold values from 0 to 16383, as said below
- suffix_len: int32 [2048], P('replica'), may hold values from 2 to 126, as said below
- prompt_key_value: bfloat16 [128, 64, 2, 1024], P('replica', None, None, 'tensor'), may hold values from -6 to 6
- prompt_len: int32 [128], P('replica'), may hold values from 2 to 64, as said below
- sibling_group: int32 [2048], P('replica'), may hold values from 0 to 127, as said below
- new_position: int32 [2048], P('replica'), may hold values from 0 to 2047, as said below
- output_weight: bfloat16 [8192, 8192], P('tensor', 'replica'), may hold values from -0.25 to 0.25
Outputs:
- moved_cache: bfloat16 [2048, 128, 2, 1024], P('replica', None, None, 'tensor')
- block_output: bfloat16 [2, 2048, 8192], P(None, 'tensor', 'replica')
Inputs may be any that keep to these rules, and one draw needn't show every extreme that they name: page_table maps the pages of the siblings of replica r one to one onto pool pages r * 32 * 8 to (r + 1) * 32 * 8 - 1. `suffix_len`: lengths differ between replicas; the largest is reached. `prompt_len`: the largest is reached. `sibling_group`: A sibling at old position s lies on replica s // 32 and belongs to one of the groups r * 2 to (r + 1) * 2 - 1 of that replica r, whose prompts that replica holds; every group has at least one sibling. `new_position`: A permutation; the new position is a replica times 32 plus a slot. The 32 siblings of one replica go to 32 different replicas, and every replica receives exactly 32. `queries`: real values of order one. `fresh_entries`: real values of order one.
All inputs are finite; a program needn't handle non-finite values.
Results may differ from a plain program's by a relative error of at most 0.02.
Values may be sent and summed in bfloat16 or wider, within the bound.
A program may use at most 64 MiB of HBM per device.

v0:
```python
import math

import jax
import jax.numpy as jnp
from jax import lax
from jax.sharding import PartitionSpec as P

HEAD_SIZE = 128


masked_score = -1e30


def empty_state(sibling_count, steps, kv_count, group_members, width):
    shape = (sibling_count, steps, kv_count, group_members)
    return (
        jnp.full(shape, masked_score, jnp.float32),
        jnp.zeros(shape, jnp.float32),
        jnp.zeros(shape + (width,), jnp.float32),
    )


def attend_block(running, query_row_block, key_row_block, value_row_block, visible):
    old_max, old_sums, old_weighted = running
    scores = jnp.einsum(
        "stkgd,spkd->stkgp", query_row_block, key_row_block, preferred_element_type=jnp.float32
    ) / math.sqrt(query_row_block.shape[-1])
    is_live = visible[:, :, None, None, :]
    scores = jnp.where(is_live, scores, masked_score)
    new_max = jnp.maximum(old_max, jnp.max(scores, axis=-1))
    weights = jnp.where(is_live, jnp.exp(scores - new_max[..., None]), 0.0)
    rescale = jnp.exp(old_max - new_max)
    new_sums = old_sums * rescale + jnp.sum(weights, axis=-1)
    update = jnp.einsum(
        "stkgp,spkd->stkgd",
        weights.astype(jnp.bfloat16),
        value_row_block,
        preferred_element_type=jnp.float32,
    )
    return (new_max, new_sums, old_weighted * rescale[..., None] + update)


def split_entries(block, kv_count):
    sibling_count, positions = (block.shape[0], block.shape[1])
    width = block.shape[3] // kv_count
    key_row_block = block[:, :, 0].reshape(sibling_count, positions, kv_count, width)
    value_row_block = block[:, :, 1].reshape(sibling_count, positions, kv_count, width)
    return (key_row_block, value_row_block)


def prompt_block(running, query_row_block, groups, shard_rows, shard_lengths, first_row):
    row_count = shard_rows.shape[0]
    offset = groups - first_row
    in_shard = (offset >= 0) & (offset < row_count)
    offset = jnp.clip(offset, 0, row_count - 1)
    chosen = jnp.take(shard_rows, offset, axis=0)
    chosen_length = jnp.take(shard_lengths, offset, axis=0)
    position = jnp.arange(chosen.shape[1], dtype=jnp.int32)
    visible = in_shard[:, None] & (position[None, :] < chosen_length[:, None])
    visible = jnp.broadcast_to(
        visible[:, None, :], (chosen.shape[0], query_row_block.shape[1], chosen.shape[1])
    )
    key_row_block, value_row_block = split_entries(chosen, query_row_block.shape[2])
    return attend_block(running, query_row_block, key_row_block, value_row_block, visible)


def suffix_block(running, query_row_block, suffix_cache, lengths):
    position = jnp.arange(suffix_cache.shape[1], dtype=jnp.int32)
    horizon = lengths[:, None] + 1 + jnp.arange(query_row_block.shape[1], dtype=jnp.int32)[None, :]
    visible = position[None, None, :] < horizon[:, :, None]
    key_row_block, value_row_block = split_entries(suffix_cache, query_row_block.shape[2])
    return attend_block(running, query_row_block, key_row_block, value_row_block, visible)


def finish_state(running):
    new_max, sums, weighted = running
    decode_result = weighted / sums[..., None]
    return decode_result.reshape(decode_result.shape[0], decode_result.shape[1], -1).astype(
        jnp.bfloat16
    )


def build_cache(suffix_page_pool, page_table, suffix_len, fresh_entries, first_page):
    sibling_count, page_count = page_table.shape
    pages = jnp.take(suffix_page_pool, (page_table - first_page).reshape(-1), axis=0)
    suffix_cache = pages.reshape(
        sibling_count,
        page_count * suffix_page_pool.shape[1],
        suffix_page_pool.shape[2],
        suffix_page_pool.shape[3],
    )
    position = jnp.arange(suffix_cache.shape[1], dtype=jnp.int32)[None, :]
    length = suffix_len[:, None]
    suffix_cache = jnp.where(
        (position < length)[:, :, None, None], suffix_cache, jnp.zeros((), suffix_cache.dtype)
    )
    for step_index in range(fresh_entries.shape[1]):
        fresh_spot = (position == length + step_index)[:, :, None, None]
        suffix_cache = jnp.where(fresh_spot, fresh_entries[:, step_index][:, None], suffix_cache)
    return suffix_cache


def arrival_order(arrived_position, own_first, sibling_count):
    target_slot = arrived_position - own_first
    slots = jnp.arange(sibling_count, dtype=jnp.int32)
    senders = jnp.arange(arrived_position.shape[0], dtype=jnp.int32)
    return jnp.sum(jnp.where(target_slot[None, :] == slots[:, None], senders[None, :], 0), axis=1)


def body(
    queries,
    fresh_entries,
    suffix_page_pool,
    page_table,
    suffix_len,
    prompt_key_value,
    prompt_len,
    sibling_group,
    new_position,
    output_weight,
):
    sibling_count, steps, query_width = queries.shape
    kv_count = suffix_page_pool.shape[3] // HEAD_SIZE
    group_members = query_width // HEAD_SIZE // kv_count
    replicas = lax.axis_size("replica")
    own_index = lax.axis_index("replica")
    own_cache = build_cache(
        suffix_page_pool,
        page_table,
        suffix_len,
        fresh_entries,
        own_index * suffix_page_pool.shape[0],
    )
    target = new_position // sibling_count
    peers = jnp.arange(replicas, dtype=jnp.int32)
    matches = target[None, :] == peers[:, None]
    present = jnp.any(matches, axis=1)
    source = jnp.sum(
        jnp.where(matches, jnp.arange(sibling_count, dtype=jnp.int32)[None, :], 0), axis=1
    )
    send_cache = jnp.where(
        present[:, None, None, None],
        jnp.take(own_cache, source, axis=0),
        jnp.zeros((), own_cache.dtype),
    )
    send_position = jnp.where(present, jnp.take(new_position, source), -1)
    own_first = own_index * sibling_count
    fresh_state = empty_state(sibling_count, steps, kv_count, group_members, HEAD_SIZE)
    send_query = jnp.take(queries, source, axis=0)
    send_facts = jnp.stack(
        [send_position, jnp.take(suffix_len, source), jnp.take(sibling_group, source)], axis=1
    )
    got_cache, got_query, got_facts = (
        lax.all_to_all(send_cache, "replica", split_axis=0, concat_axis=0, tiled=True),
        lax.all_to_all(send_query, "replica", split_axis=0, concat_axis=0, tiled=True),
        lax.all_to_all(send_facts, "replica", split_axis=0, concat_axis=0, tiled=True),
    )
    arrivals = arrival_order(got_facts[:, 0], own_first, sibling_count)
    moved_cache = jnp.take(got_cache, arrivals, axis=0)
    query_row_block = jnp.take(got_query, arrivals, axis=0).reshape(
        sibling_count, steps, kv_count, group_members, HEAD_SIZE
    )
    facts = jnp.take(got_facts, arrivals, axis=0)
    groups = facts[:, 2]
    shard_rows = (
        lax.all_gather(prompt_key_value, "replica", axis=0, tiled=True),
        lax.all_gather(prompt_len, "replica", axis=0, tiled=True),
    )
    running = prompt_block(
        fresh_state, query_row_block, groups, shard_rows[0], shard_rows[1], jnp.int32(0)
    )
    running = suffix_block(running, query_row_block, moved_cache, facts[:, 1])
    attended = finish_state(running)
    shard_rows = lax.all_gather(attended, "replica", axis=0, tiled=True)
    row_count = shard_rows.shape[0]
    flattened = shard_rows.reshape(row_count * steps, shard_rows.shape[2])
    partial_terms = jnp.dot(flattened, output_weight, preferred_element_type=jnp.float32)
    terms = partial_terms.reshape(row_count, steps, -1).transpose(1, 0, 2)
    block_output = lax.psum_scatter(
        terms.astype(jnp.bfloat16), "tensor", scatter_dimension=1, tiled=True
    )
    return (moved_cache, block_output)


def solution(mesh):
    placed = (
        P("replica", None, "tensor"),
        P("replica", None, None, "tensor"),
        P("replica", None, None, "tensor"),
        P("replica", None),
        P("replica"),
        P("replica", None, None, "tensor"),
        P("replica"),
        P("replica"),
        P("replica"),
        P("tensor", "replica"),
    )
    return jax.shard_map(
        body,
        mesh=mesh,
        in_specs=placed,
        out_specs=(P("replica", None, None, "tensor"), P(None, "tensor", "replica")),
        check_vma=False,
    )
```

profile of v0, /device:TPU:1, one launch (start us, length us, event | category | flops | bytes accessed | tf_op | source)
XLA Modules:
  0.0 534.0 jit_solution(2130132839417917710)
XLA Ops:
  8.2 1.4 gather_fusion.8
  9.6 1.4 gather_fusion.10
  11.1 1.4 gather_fusion.9
  13.2 19.1 %all-to-all-start = ((s32[64,1,3]{2,1,0:T(1,128)}), s32[64,1,3]{2,1,0:T(1,128)S(1)}, u32[]{:S(2)}, u32[]{:S(2)}) async-start(s32[64,1,3]{2,1,0:T(1,128)} %bitcast.3), calls=%async_computation | async-start | bytes 65536 | tf_op jit(solution)/shard_map/all_to_all | solution.py:156
  34.7 2.0 gather_fusion.6
  36.7 1.1 broadcast_select_fusion
  37.9 10.5 %gather_fusion = bf16[256,16,2,128]{3,2,1,0:T(2,128)(2,1)} fusion(bf16[256,16,2,128]{3,2,1,0:T(2,128)(2,1)S(1)} %copy-done, s32[1024]{0:T(1024)S(1)} %pad_clamp_fusion.3), kind=kCustom, calls=%fused_computation.3 | custom fusion | bytes 4195328 | tf_op jit(solution)/shard_map/jit(_take)/gather | solution.py:85
  48.4 3.2 copy.63
  51.6 14.5 %all-to-all-start.2 = ((bf16[64,2,1024]{2,1,0:T(2,128)(2,1)}), bf16[64,2,1024]{2,1,0:T(2,128)(2,1)S(1)}, u32[]{:S(2)}, u32[]{:S(2)}) async-start(bf16[64,2,1024]{2,1,0:T(2,128)(2,1)} %broadcast_select_fusion), calls=%async_computation.2 | async-start | bytes 524288 | tf_op jit(solution)/shard_map/all_to_all | solution.py:155
  66.2 6.9 %fusion.3 = bf16[32,128,2,128]{3,1,0,2:T(8,128)(2,1)} fusion(pred[32,128]{1,0:T(8,128)(4,1)S(1)} %copy.61, pred[32,128]{1,0:T(8,128)(4,1)S(1)} %get-tuple-element.29, pred[32,128]{1,0:T(8,128)(4,1)S(1)} %get-tuple-element.28, pred[32,128]{1,0:T(8,128)(4,1)S(1)} %get-tuple-element.34, bf16[32,2,128]{2,0,1:T(8,128)(2,1)S(1)} %copy.60, ...), kind=kLoop, calls=%fused_computation.17 | loop fusion | flops 4194304 | bytes 4243456 | tf_op jit(solution)/shard_map/jit(_where)/select_n | solution.py:99
  73.1 4.6 gather_fusion.1
  77.7 4.0 select_select_fusion
  81.7 3.0 all-to-all-done.2
  84.8 11.9 %all-to-all-start.1 = ((bf16[64,128,2,128]{3,1,2,0:T(8,128)(2,1)}), bf16[64,128,2,128]{3,1,2,0:T(8,128)(2,1)}, u32[]{:S(2)}, u32[]{:S(2)}) async-start(bf16[64,128,2,128]{3,1,2,0:T(8,128)(2,1)} %select_select_fusion), calls=%async_computation.1 | async-start | bytes 8388608 | tf_op jit(solution)/shard_map/all_to_all | solution.py:154
  97.5 1.3 dynamic-slice
  99.7 210.2 %all-reduce = s32[128]{0:T(128)S(1)} all-reduce(s32[128]{0:T(128)S(1)} %dynamic-update-slice), channel_id=1, replica_groups=mesh['replica'=64,'tensor'=8] {'replica'}, use_global_device_ids=true, to_apply=%add | all-reduce | flops 128 | bytes 1024
  313.7 2.9 gather_fusion.5
  316.8 1.0 copy-done.3
  318.3 4.3 gather_fusion.2
  322.6 1.8 copy_select_fusion
  328.1 151.6 %all-gather.5.cloned.1.call-done = bf16[2048,2,1024]{2,0,1:T(8,128)(2,1)} async-done(((bf16[32,2,1024]{2,0,1:T(8,128)(2,1)}), bf16[2048,2,1024]{2,0,1:T(8,128)(2,1)}) %all-gather.5.cloned.1.call-update) | async-done | bytes 8388624 | tf_op jit(solution)/shard_map/all_gather | solution.py:174
  479.7 6.7 %fusion = bf16[2,2048,128]{2,1,0:T(8,128)(2,1)} fusion(bf16[2048,2,1024]{2,0,1:T(8,128)(2,1)} %all-gather.5.cloned.1.call-done, bf16[1024,128]{1,0:T(8,128)(2,1)S(1)} %copy-done.6), kind=kOutput, calls=%fused_computation.13 | convolution fusion | flops 1074266112 | bytes 9699328 | tf_op jit(solution)/shard_map/dot_general | solution.py:177
  486.4 5.1 copy.72
  491.5 35.9 %reduce-scatter.2.cloned.1.call-done = bf16[2,256,128]{2,1,0:T(8,128)(2,1)} async-done(((bf16[2,2048,128]{2,1,0:T(8,128)(2,1)}), bf16[2,256,128]{2,1,0:T(8,128)(2,1)}) %reduce-scatter.2.cloned.1.call-update) | async-done | bytes 131088 | tf_op jit(solution)/shard_map/reduce_scatter | solution.py:179
  (81 shorter events, 13.2 us)
Async XLA Ops:
  7.2 30.7 %copy-start = (bf16[256,16,2,128]{3,2,1,0:T(2,128)(2,1)S(1)}, bf16[256,16,2,128]{3,2,1,0:T(2,128)(2,1)}, u32[]{:S(2)}) copy-start(bf16[256,16,2,128]{3,2,1,0:T(2,128)(2,1)} %param.14) | copy-start | bytes 6291460
  13.2 38.3 %all-to-all-start = ((s32[64,1,3]{2,1,0:T(1,128)}), s32[64,1,3]{2,1,0:T(1,128)S(1)}, u32[]{:S(2)}, u32[]{:S(2)}) async-start(s32[64,1,3]{2,1,0:T(1,128)} %bitcast.3), calls=%async_computation | async-start | bytes 65536 | tf_op jit(solution)/shard_map/all_to_all | solution.py:156
  48.4 17.8 %copy-start.1 = (s32[32]{0:T(128)S(1)}, s32[32]{0:T(128)}, u32[]{:S(2)}) copy-start(s32[32]{0:T(128)} %param.16) | copy-start | bytes 388
  51.6 33.2 %all-to-all-start.2 = ((bf16[64,2,1024]{2,1,0:T(2,128)(2,1)}), bf16[64,2,1024]{2,1,0:T(2,128)(2,1)S(1)}, u32[]{:S(2)}, u32[]{:S(2)}) async-start(bf16[64,2,1024]{2,1,0:T(2,128)(2,1)} %broadcast_select_fusion), calls=%async_computation.2 | async-start | bytes 524288 | tf_op jit(solution)/shard_map/all_to_all | solution.py:155
  81.7 15.0 %copy-start.5 = (bf16[2,64,2,128]{3,2,1,0:T(2,128)(2,1)S(1)}, bf16[2,64,2,128]{3,2,1,0:T(2,128)(2,1)}, u32[]{:S(2)}) copy-start(bf16[2,64,2,128]{3,2,1,0:T(2,128)(2,1)} %param.17) | copy-start | bytes 196612
  81.7 17.7 %copy-start.7 = (s32[2]{0:T(128)S(1)}, s32[2]{0:T(128)}, u32[]{:S(2)}) copy-start(s32[2]{0:T(128)} %param.18) | copy-start | bytes 28
  84.8 233.5 %all-to-all-start.1 = ((bf16[64,128,2,128]{3,1,2,0:T(8,128)(2,1)}), bf16[64,128,2,128]{3,1,2,0:T(8,128)(2,1)}, u32[]{:S(2)}, u32[]{:S(2)}) async-start(bf16[64,128,2,128]{3,1,2,0:T(8,128)(2,1)} %select_select_fusion), calls=%async_computation.1 | async-start | bytes 8388608 | tf_op jit(solution)/shard_map/all_to_all | solution.py:154
  96.7 217.0 %all-gather.3.cloned.1.call-start = ((), (), s32[]{:S(2)}) async-start(), calls=%async_computation.4 | async-start | bytes 4259840 | tf_op jit(solution)/shard_map/all_gather | solution.py:166
  97.4 382.2 %all-gather.5.cloned.1.call-start = ((), (), s32[]{:S(2)}) async-start(), calls=%async_computation.5 | async-start | bytes 8519680 | tf_op jit(solution)/shard_map/all_gather | solution.py:174
  316.8 1.0 copy-start.3
  324.5 2.3 copy-start.2
  324.5 2.0 copy-start.4
  326.8 152.9 %copy-start.6 = (bf16[1024,128]{1,0:T(8,128)(2,1)S(1)}, bf16[1024,128]{1,0:T(8,128)(2,1)}, u32[]{:S(2)}) copy-start(bf16[1024,128]{1,0:T(8,128)(2,1)} %param.21) | copy-start | bytes 786436
  328.0 199.4 %reduce-scatter.2.cloned.1.call-start = ((), (), s32[]{:S(2)}) async-start(), calls=%async_computation.6 | async-start | bytes 1179648 | tf_op jit(solution)/shard_map/reduce_scatter | solution.py:179
Sparse Core Ops, SparseCore 0:
  101.0 212.5 all-gather.2
  328.1 151.4 all-gather.4
  486.5 40.8 reduce-scatter.1
where the time goes:
time: 536 us; the launch traced here: 534 us
  blocking collectives  210 us (39%)
  waiting for transfers between devices  191 us (36%)
  starting transfers between devices  45.7 us (9%)
  local copies, waits for them, and re-layouts  45.4 us (8%)
  other arithmetic  18.5 us (3%)
  between operations  14.8 us (3%)
  matrix products  8.79 us (2%)
    unnamed x1, blocking collectives  210 us
    all_gather x1, waiting for transfers between devices, body(): shard_rows = lax.all_gather(attended, 'replica', axis=0, tiled=True)  152 us
    reduce_scatter x1, waiting for transfers between devices, body(): lax.psum_scatter(terms.astype(jnp.bfloat16), 'tensor', scatter_dimension=...  35.9 us
    all_to_all x1, starting transfers between devices, body(): lax.all_to_all(send_facts, 'replica', split_axis=0, concat_axis=0, tiled=...  19.1 us
    all_to_all x1, starting transfers between devices, body(): lax.all_to_all(send_query, 'replica', split_axis=0, concat_axis=0, tiled=...  14.5 us
    gather x2, local copies, waits for them, and re-layouts, build_cache(): jnp.take(suffix_page_pool, (page_table - first_page).reshape(-1), axis=0)  13.7 us
    all_to_all x1, starting transfers between devices, body(): lax.all_to_all(send_cache, 'replica', split_axis=0, concat_axis=0, tiled=...  11.9 us
  transfers between devices with their start and end apart: 6, of which 3 were waited for; matrix products, arithmetic and copies ran while one was open for 9% of the time, Pallas kernels for 0%

commit v1 on v0

v1 whole, which is shorter than its diff:
```python
import functools
import math

import jax
import jax.numpy as jnp
from jax import lax
from jax.experimental import pallas as pl
from jax.experimental.pallas import tpu as pltpu
from jax.sharding import PartitionSpec as P

MESH = pl.DeviceIdType.MESH
BF16, F32, I32 = jnp.bfloat16, jnp.float32, jnp.int32
HEAD = 128
X, Z, T = 4, 16, 8
S = 32
UNITS = 16
LANE_UNITS = UNITS // X
CAPACITIES = (28, 64)
masked_score = -1e30

VM = pl.BlockSpec(memory_space=pltpu.VMEM)
SM = pl.BlockSpec(memory_space=pltpu.SMEM)


def place():
    r = lax.axis_index("replica")
    return r // X, lax.rem(r, X), lax.axis_index("tensor")


def to_replica(z, x):
    return dict(device_id={"replica": z * X + x}, device_id_type=MESH)


def to_tensor(t):
    return dict(device_id={"tensor": t}, device_id_type=MESH)


def attend_kernel(
    page_ref, len_ref, slot_ref, group_ref, plen_ref,
    facts_ref, pool_ref, query_ref, fresh_ref, prompt_ref, weight_ref,
    all_facts_ref, xbuf_ref, gathered_ref, wide_ref,
    cache, split, heads, fresh32, f_send, f_recv, g_send, g_recv,
    x_send, x_recv, w_send, w_recv, r_send, r_recv, l_send, l_recv, own_sem,
):
    z, x, _ = place()
    up, down = lax.rem(z + 1, Z), lax.rem(z + Z - 1, Z)
    barrier = pltpu.get_barrier_semaphore()
    for i in range(1, X):
        pl.semaphore_signal(barrier, inc=1, **to_replica(z, lax.rem(x + i, X)))

    @pl.loop(1, Z)
    def _(i):
        pl.semaphore_signal(barrier, inc=1, **to_replica(lax.rem(z + i, Z), x))

    mine = all_facts_ref.at[z, pl.ds(x, 1)]
    all_facts_ref[z, pl.ds(x, 1)] = facts_ref[...]
    pl.semaphore_wait(barrier, X + Z - 2)

    def f_copy(i):
        return pltpu.make_async_remote_copy(
            mine, mine, f_send.at[i], f_recv.at[i], **to_replica(z, lax.rem(x + i, X))
        )

    def g_copy(i):
        return pltpu.make_async_remote_copy(
            all_facts_ref.at[z], all_facts_ref.at[z], g_send.at[i], g_recv.at[i], **to_replica(lax.rem(z + i, Z), x)
        )

    for i in range(1, X):
        f_copy(i).start()

    fresh32[...] = fresh_ref[...].astype(F32)
    row = lax.broadcasted_iota(I32, (16, HEAD), 0)
    odd = lax.rem(row, 2) == 1
    token_of_row = row // 2

    @pl.loop(0, S)
    def _(s):
        length = len_ref[s]
        one = jnp.where(odd, fresh32[pl.ds(4 * s + 1, 1), :], fresh32[pl.ds(4 * s, 1), :])
        two = jnp.where(odd, fresh32[pl.ds(4 * s + 3, 1), :], fresh32[pl.ds(4 * s + 2, 1), :])
        for page in range(8):
            source = page_ref[s * 8 + page]
            for half in range(2):
                unit = pool_ref[source, 16 * half : 16 * (half + 1), :].astype(F32)
                token = token_of_row + (16 * page + 8 * half) - length
                unit = jnp.where(
                    token < 0, unit, jnp.where(token == 0, one, jnp.where(token == 1, two, 0.0))
                )
                cache[s, 2 * page + half] = unit.astype(BF16)

    @pl.loop(0, S)
    def _(s):
        slot = slot_ref[s]
        for lane in range(X):
            turn = lax.rem(lane + 4 * S - lax.rem(slot, 4), 4)
            for k in range(LANE_UNITS):
                split[lane, s, k] = cache[s, 4 * k + turn]

    def x_copy(i):
        lane = lax.rem(x + i, X)
        return pltpu.make_async_remote_copy(
            split.at[lane], xbuf_ref.at[x], x_send.at[i], x_recv.at[i], **to_replica(z, lane)
        )

    def w_copy(i):
        return pltpu.make_async_remote_copy(
            weight_ref, wide_ref.at[x], w_send.at[i], w_recv.at[i], **to_replica(z, lax.rem(x + i, X))
        )

    for i in range(1, X):
        x_copy(i).start()
    for i in range(1, X):
        w_copy(i).start()
    own_split = pltpu.make_async_copy(split.at[x], xbuf_ref.at[x], own_sem.at[0])
    own_weight = pltpu.make_async_copy(weight_ref, wide_ref.at[x], own_sem.at[1])
    own_split.start()
    own_weight.start()
    for i in range(1, X):
        f_copy(i).wait()

    @pl.loop(1, Z)
    def _(i):
        g_copy(i).start()

    scale = 1.0 / math.sqrt(HEAD)
    column = lax.broadcasted_iota(I32, (16, 256), 1)
    step = lax.rem(lax.broadcasted_iota(I32, (16, 256), 0), 2)
    suffix_token = column // 2 - 1 - step
    is_key = lax.rem(column, 2) == 0
    pcolumn = lax.broadcasted_iota(I32, (16, HEAD), 1)
    is_pkey = lax.rem(pcolumn, 2) == 0
    by_column = (((1,), (1,)), ((), ()))

    def attend(s):
        query = query_ref[s]
        group = lax.rem(group_ref[s], 2)
        prompt = prompt_ref[group]
        entries = cache[s].reshape(256, HEAD)
        seen = is_key & (suffix_token < len_ref[s])
        pseen = is_pkey & (pcolumn // 2 < plen_ref[group])
        scores = lax.dot_general(query, entries, by_column, preferred_element_type=F32) * scale
        pscores = lax.dot_general(query, prompt, by_column, preferred_element_type=F32) * scale
        scores = jnp.where(seen, scores, masked_score)
        pscores = jnp.where(pseen, pscores, masked_score)
        top = jnp.maximum(
            jnp.max(scores, axis=1, keepdims=True), jnp.max(pscores, axis=1, keepdims=True)
        )
        weights = jnp.where(seen, jnp.exp(scores - top), 0.0)
        pweights = jnp.where(pseen, jnp.exp(pscores - top), 0.0)
        total = jnp.sum(weights, axis=1, keepdims=True) + jnp.sum(pweights, axis=1, keepdims=True)
        weights = pltpu.roll(weights, 1, 1).astype(BF16)
        pweights = pltpu.roll(pweights, 1, 1).astype(BF16)
        out = jnp.dot(weights, entries, preferred_element_type=F32)
        out = out + jnp.dot(pweights, prompt, preferred_element_type=F32)
        return out / total

    @pl.loop(0, S // 4)
    def _(block):
        outs = [attend(4 * block + i) for i in range(4)]
        for i, out in enumerate(outs):
            for head in range(8):
                for k in range(2):
                    heads[head, pl.ds(k * S + 4 * block + i, 1), :] = out[2 * head + k : 2 * head + k + 1]

    gathered_ref[z] = heads[...].astype(BF16)

    def ring(step, part, forward):
        plane = lax.rem(z + Z - step, Z) if forward else lax.rem(z + step, Z)
        block = gathered_ref.at[plane, pl.ds(4 * part, 4)]
        send, recv = (r_send, r_recv) if forward else (l_send, l_recv)
        return pltpu.make_async_remote_copy(
            block, block, send.at[2 * step + part], recv.at[2 * step + part],
            **to_replica(up if forward else down, x),
        )

    for step in range(Z // 2):
        for part in range(2):
            for forward in (True, False):
                if not forward and step == Z // 2 - 1:
                    continue
                if step:
                    ring(step - 1, part, forward).wait_recv()
                ring(step, part, forward).start()
    for part in range(2):
        ring(Z // 2 - 1, part, True).wait_recv()
        ring(Z // 2 - 2, part, False).wait_recv()
    for step in range(Z // 2):
        for part in range(2):
            for forward in (True, False):
                if not forward and step == Z // 2 - 1:
                    continue
                ring(step, part, forward).wait_send()

    @pl.loop(1, Z)
    def _(i):
        g_copy(i).wait()

    for i in range(1, X):
        w_copy(i).wait()
    for i in range(1, X):
        x_copy(i).wait()
    own_split.wait()
    own_weight.wait()


def attend_call(pages, length, slot, group, plen, facts, pool, query, fresh, prompt, weight):
    half = Z // 2
    return pl.pallas_call(
        attend_kernel,
        out_shape=(
            jax.ShapeDtypeStruct((Z, X, 1, HEAD), I32),
            jax.ShapeDtypeStruct((X, S, LANE_UNITS, 16, HEAD), BF16),
            jax.ShapeDtypeStruct((Z, 8, 2 * S, HEAD), BF16),
            jax.ShapeDtypeStruct((X,) + weight.shape, BF16),
        ),
        in_specs=[SM] * 5 + [VM] * 6,
        out_specs=(VM, VM, VM, VM),
        scratch_shapes=[
            pltpu.VMEM((S, UNITS, 16, HEAD), BF16),
            pltpu.VMEM((X, S, LANE_UNITS, 16, HEAD), BF16),
            pltpu.VMEM((8, 2 * S, HEAD), F32),
            pltpu.VMEM((4 * S, HEAD), F32),
            pltpu.SemaphoreType.DMA((X,)),
            pltpu.SemaphoreType.DMA((X,)),
            pltpu.SemaphoreType.DMA((Z,)),
            pltpu.SemaphoreType.DMA((Z,)),
            pltpu.SemaphoreType.DMA((X,)),
            pltpu.SemaphoreType.DMA((X,)),
            pltpu.SemaphoreType.DMA((X,)),
            pltpu.SemaphoreType.DMA((X,)),
            pltpu.SemaphoreType.DMA((2 * half,)),
            pltpu.SemaphoreType.DMA((2 * half,)),
            pltpu.SemaphoreType.DMA((2 * half,)),
            pltpu.SemaphoreType.DMA((2 * half,)),
            pltpu.SemaphoreType.DMA((2,)),
        ],
        compiler_params=pltpu.CompilerParams(
            collective_id=1, has_side_effects=True, vmem_limit_bytes=40 << 20
        ),
        name="attend_and_gather",
    )(pages, length, slot, group, plen, facts, pool, query, fresh, prompt, weight)


def move_kernel(
    capacity,
    pack_ref, unpack_ref, position_ref, xbuf_ref, gathered_ref, wide_ref,
    moved_ref, block_ref,
    packed, arrived, product, columns, chunk, chunks, deliver,
    z_send, z_recv, c_send, c_recv, t_send, t_recv, d_send, d_recv, own_sem,
):
    z, x, t = place()
    barrier = pltpu.get_barrier_semaphore()

    @pl.loop(1, Z)
    def _(i):
        pl.semaphore_signal(barrier, inc=1, **to_replica(lax.rem(z + i, Z), x))

    for i in range(1, X):
        pl.semaphore_signal(barrier, inc=1, **to_replica(z, lax.rem(x + i, X)))
    for i in range(1, T):
        pl.semaphore_signal(barrier, inc=1, **to_tensor(lax.rem(t + i, T)))
    pl.semaphore_wait(barrier, Z + X + T - 3)

    def z_copy(i):
        plane = lax.rem(z + i, Z)
        return pltpu.make_async_remote_copy(
            packed.at[plane], arrived.at[z], z_send.at[i], z_recv.at[i], **to_replica(plane, x)
        )

    @pl.loop(0, Z)
    def _(i):
        plane = lax.rem(z + i, Z)
        for c in range(capacity):
            packed[plane, c] = xbuf_ref[pack_ref[plane * capacity + c]]

        @pl.when(i > 0)
        def _():
            z_copy(i).start()

    own_plane = pltpu.make_async_copy(packed.at[z], arrived.at[z], own_sem.at[0])
    own_plane.start()
    arrived[Z, 0] = jnp.zeros((16, HEAD), BF16)

    @pl.loop(0, Z // 4)
    def _(b):
        blocks = gathered_ref[pl.ds(4 * b, 4)]
        rows = jnp.concatenate([blocks[:, h].reshape(8 * S, HEAD) for h in range(8)], axis=1)
        for pair in range(X // 2):
            weight = jnp.concatenate([wide_ref[2 * pair], wide_ref[2 * pair + 1]], axis=1)
            out = jnp.dot(rows, weight, preferred_element_type=F32).astype(BF16)
            out = out.reshape(4, 2, S, 2 * HEAD)
            for i in range(2):
                for k in range(2):
                    part = out[:, k, :, i * HEAD : (i + 1) * HEAD].reshape(4 * S, HEAD)
                    product[2 * pair + i, k, pl.ds(pl.multiple_of(b * 4 * S, 4 * S), 4 * S), :] = part

    def c_copy(i):
        lane = lax.rem(x + i, X)
        return pltpu.make_async_remote_copy(
            product.at[lane], columns.at[x], c_send.at[i], c_recv.at[i], **to_replica(z, lane)
        )

    for i in range(1, X):
        c_copy(i).start()
    own_columns = pltpu.make_async_copy(product.at[x], columns.at[x], own_sem.at[1])
    own_columns.start()
    own_columns.wait()
    for i in range(1, X):
        c_copy(i).wait()

    def t_copy(i):
        other = lax.rem(t + i, T)
        return pltpu.make_async_remote_copy(
            chunk.at[other], chunks.at[t], t_send.at[i], t_recv.at[i], **to_tensor(other)
        )

    @pl.loop(0, T)
    def _(n):
        i = lax.rem(n + 1, T)
        other = lax.rem(t + i, T)
        target = lax.broadcasted_iota(I32, (8 * S, Z * S), 0) + other * (8 * S)
        total = jnp.zeros((8 * S, 2 * HEAD), F32)
        for lane in range(X):
            pick = (position_ref[pl.ds(lane, 1), :] == target).astype(F32).astype(BF16)
            rows = jnp.concatenate([columns[lane, 0], columns[lane, 1]], axis=1)
            total = total + jnp.dot(pick, rows, preferred_element_type=F32)
        for k in range(2):
            chunk[other, k] = total[:, k * HEAD : (k + 1) * HEAD].astype(BF16)

        @pl.when(i > 0)
        def _():
            t_copy(i).start()

    own_chunk = pltpu.make_async_copy(chunk.at[t], chunks.at[t], own_sem.at[2])
    own_chunk.start()
    own_chunk.wait()
    for i in range(1, T):
        t_copy(i).wait()
    for k in range(2):
        total = chunks[0, k].astype(F32)
        for n in range(1, T):
            total = total + chunks[n, k].astype(F32)
        block_ref[k] = total.astype(BF16)

    own_plane.wait()

    @pl.loop(1, Z)
    def _(i):
        z_copy(i).wait()

    flat = arrived.at[...]

    def d_copy(i, turn):
        lane = lax.rem(x + i, X)
        return pltpu.make_async_remote_copy(
            deliver.at[lane, :, turn], moved_ref.at[:, turn, :, lax.rem(x + X - turn, X)],
            d_send.at[i, turn], d_recv.at[i, turn], **to_replica(z, lane),
        )

    def own_deliver(turn):
        return pltpu.make_async_copy(
            deliver.at[x, :, turn], moved_ref.at[:, turn, :, lax.rem(x + X - turn, X)], own_sem.at[turn + 3]
        )

    @pl.loop(0, X)
    def _(n):
        i = lax.rem(n + 1, X)
        lane = lax.rem(x + i, X)

        @pl.loop(0, S // 4)
        def _(s):
            for turn in range(4):
                for k in range(LANE_UNITS):
                    index = unpack_ref[((lane * (S // 4) + s) * 4 + turn) * LANE_UNITS + k]
                    deliver[lane, s, turn, k] = flat[index // capacity, lax.rem(index, capacity)]

        @pl.when(i > 0)
        def _():
            for turn in range(4):
                d_copy(i, turn).start()

    for turn in range(4):
        own_deliver(turn).start()
    for turn in range(4):
        own_deliver(turn).wait()
    for i in range(1, X):
        for turn in range(4):
            d_copy(i, turn).wait()


def move_call(number, capacity, pack, unpack, position, xbuf, gathered, wide):
    dma = pltpu.SemaphoreType.DMA
    return pl.pallas_call(
        functools.partial(move_kernel, capacity),
        out_shape=(
            jax.ShapeDtypeStruct((S // 4, 4, LANE_UNITS, X, 16, HEAD), BF16),
            jax.ShapeDtypeStruct((2, 8 * S, HEAD), BF16),
        ),
        in_specs=[SM, SM, VM, VM, VM, VM],
        out_specs=(VM, VM),
        scratch_shapes=[
            pltpu.VMEM((Z, capacity, 16, HEAD), BF16),
            pltpu.VMEM((Z + 1, capacity, 16, HEAD), BF16),
            pltpu.VMEM((X, 2, Z * S, HEAD), BF16),
            pltpu.VMEM((X, 2, Z * S, HEAD), BF16),
            pltpu.VMEM((T, 2, 8 * S, HEAD), BF16),
            pltpu.VMEM((T, 2, 8 * S, HEAD), BF16),
            pltpu.VMEM((X, S // 4, 4, LANE_UNITS, 16, HEAD), BF16),
            dma((Z,)), dma((Z,)), dma((X,)), dma((X,)), dma((T,)), dma((T,)),
            dma((X, 4)), dma((X, 4)), dma((7,)),
        ],
        compiler_params=pltpu.CompilerParams(
            collective_id=2 + number, has_side_effects=True, vmem_limit_bytes=48 << 20
        ),
        name="move_and_project",
    )(pack, unpack, position, xbuf, gathered, wide)


def body(
    queries, fresh_entries, suffix_page_pool, page_table, suffix_len,
    prompt_key_value, prompt_len, sibling_group, new_position, output_weight,
):
    z, x, _ = place()
    facts = jnp.concatenate([new_position, suffix_len, jnp.zeros((2 * S,), I32)]).reshape(1, 1, HEAD)
    query = queries.reshape(S, 2, 8, HEAD).transpose(0, 2, 1, 3).reshape(S, 16, HEAD)
    facts, xbuf, gathered, wide = attend_call(
        page_table.reshape(-1) - (z * X + x) * (S * 8), suffix_len, new_position, sibling_group, prompt_len, facts,
        suffix_page_pool.reshape(S * 8, 32, HEAD), query, fresh_entries.reshape(4 * S, HEAD),
        prompt_key_value.reshape(2, 2 * 64, HEAD), output_weight,
    )

    position = facts[:, :, 0, :S].reshape(Z, X * S)
    tokens = facts[:, :, 0, S : 2 * S].reshape(Z, X * S) + 2
    plane = position // (X * S)
    filled = (tokens + 7) // 8
    lanes = jnp.arange(X, dtype=I32)
    turn = (lanes[:, None, None] - position[None]) % 4
    counts = (filled[None] - turn + 3) // 4
    planes = jnp.arange(Z, dtype=I32)
    load = jnp.sum(
        jnp.where(plane[None, :, None, :] == planes[None, None, :, None], counts[:, :, None, :], 0), axis=3
    )
    largest = jnp.max(load)
    count = jnp.sum(jnp.where((lanes == x)[:, None, None], counts, 0), axis=0)
    members = jnp.arange(X * S, dtype=I32)
    ahead = (plane[:, :, None] == plane[:, None, :]) & (members[None, None, :] < members[None, :, None])
    offset = jnp.sum(jnp.where(ahead, count[:, None, :], 0), axis=2)

    unit = jnp.arange(LANE_UNITS, dtype=I32)
    own = lambda a: lax.dynamic_index_in_dim(a, z, 0, keepdims=False)
    own_count, own_offset, own_plane = own(count), own(offset), own(plane)
    wanted = z * (X * S) + members
    match = (position.reshape(-1)[None, :] == wanted[:, None])
    find = lambda a: jnp.sum(jnp.where(match, a.reshape(-1)[None, :], 0), axis=1)
    from_plane = find(jnp.broadcast_to(planes[:, None], plane.shape))
    from_offset, from_count = find(offset), find(count)
    by_lane = position.reshape(Z, X, S).transpose(1, 0, 2).reshape(X, Z * S)

    def branch(number, capacity):
        def run(xbuf, gathered, wide):
            spot = own_plane[:, None] * capacity + own_offset[:, None] + unit[None, :]
            spot = jnp.where(unit[None, :] < own_count[:, None], spot, -1).reshape(-1)
            spots = jnp.arange(Z * capacity, dtype=I32)
            pack = jnp.sum(
                jnp.where(spot[None, :] == spots[:, None], jnp.arange(spot.shape[0], dtype=I32)[None, :], 0), axis=1
            )
            start = from_plane * capacity + from_offset
            unpack = jnp.where(
                unit[None, :] < from_count[:, None], start[:, None] + unit[None, :], Z * capacity
            ).reshape(-1)
            return move_call(number, capacity, pack, unpack, by_lane, xbuf, gathered, wide)

        return run

    small = sum((largest > c).astype(I32) for c in CAPACITIES[:-1])
    moved, block = lax.switch(
        small, [branch(n, c) for n, c in enumerate(CAPACITIES)],
        xbuf.reshape(X * S * LANE_UNITS, 16, HEAD), gathered, wide,
    )
    return moved.reshape(S, 128, 2, HEAD), block


def solution(mesh):
    placed = (
        P("replica", None, "tensor"),
        P("replica", None, None, "tensor"),
        P("replica", None, None, "tensor"),
        P("replica", None),
        P("replica"),
        P("replica", None, None, "tensor"),
        P("replica"),
        P("replica"),
        P("replica"),
        P("tensor", "replica"),
    )
    return jax.shard_map(
        body,
        mesh=mesh,
        in_specs=placed,
        out_specs=(P("replica", None, None, "tensor"), P(None, "tensor", "replica")),
        check_vma=False,
    )
```

time: 536 us -> 196 us (0.37)
  blocking collectives: 210 us -> 0 us
  waiting for transfers between devices: 191 us -> 0 us
  Pallas kernels: 0 us -> 177 us
  starting transfers between devices: 45.7 us -> 0 us
  local copies, waits for them, and re-layouts: 45.4 us -> 10.5 us
  between operations: 14.8 us -> 1.43 us
  other arithmetic: 18.5 us -> 5.45 us
  matrix products: 8.79 us -> 0 us
    unnamed x1 -> x0, blocking collectives: 210 us -> none
    pallas_call x0 -> x2, Pallas kernels: none -> 177 us  [the longest x1 117 us: move_call(): pl.pallas_call(functools.partial(move_kernel, capacity), out_shape=(jax.S...]
    all_gather x2 -> x0, waiting for transfers between devices: 152 us -> none  [the longest x1 152 us: body(): shard_rows = lax.all_gather(attended, 'replica', axis=0, tiled=True)]
    all_to_all x3 -> x0, starting transfers between devices: 45.5 us -> none  [the longest x1 19.1 us: body(): lax.all_to_all(send_facts, 'replica', split_axis=0, concat_axis=0, tiled=...]
    reduce_scatter x1 -> x0, waiting for transfers between devices: 35.9 us -> none  [body(): lax.psum_scatter(terms.astype(jnp.bfloat16), 'tensor', scatter_dimension=...]
    gather x14 -> x0, local copies, waits for them, and re-layouts: 34.2 us -> none  [the longest x2 13.7 us: build_cache(): jnp.take(suffix_page_pool, (page_table - first_page).reshape(-1), axis=0)]
    select_n x12 -> x2, other arithmetic: 15.1 us -> 0.15 us  [the longest x1 0.13 us: run(): jnp.where(unit[None, :] < from_count[:, None], start[:, None] + unit[None...]
    dot_general x5 -> x0, matrix products: 8.79 us -> none  [the longest x1 6.7 us: body(): jnp.dot(flattened, output_weight, preferred_element_type=jnp.float32)]
  transfers between devices with their start and end apart: 6 -> 0, of which waited for: 3 -> 0; matrix products, arithmetic and copies ran while one was open for 9% -> 0% of each run, Pallas kernels for 0% -> 0%
where the time goes in v1:
time: 196 us; the launch traced here: 194 us
  Pallas kernels  177 us (90%)
  local copies, waits for them, and re-layouts  10.5 us (5%)
  other arithmetic  5.45 us (3%)
    pallas_call x1, Pallas kernels, move_call(): pl.pallas_call(functools.partial(move_kernel, capacity), out_shape=(jax.S...  117 us
    pallas_call x1, Pallas kernels, attend_call(): pl.pallas_call(attend_kernel, out_shape=(jax.ShapeDtypeStruct((Z, X, 1, H...  59.6 us
    unnamed x20, local copies, waits for them, and re-layouts  9.63 us

profile of v1, /device:TPU:1, one launch (start us, length us, event | category | flops | bytes accessed | tf_op | source)
XLA Modules:
  0.0 194.1 jit_solution(3442341841920960018)
XLA Ops:
  0.7 0.8 add_bitcast_fusion.facts_ref
  1.4 0.7 broadcast_subtract_fusion
  2.3 1.6 copy-done
  3.9 0.9 copy-done.1
  4.9 0.9 copy-done.2
  5.8 0.8 copy-done.3
  6.6 0.8 copy-done.4
  7.4 0.7 copy-done.5
  8.0 0.7 copy-done.6
  8.7 0.7 copy-done.7
  9.3 0.7 copy-done.8
  10.0 59.6 %attend_and_gather.1 = (s32[16,4,1,128]{3,2,1,0:T(1,128)S(1)}, bf16[4,32,4,16,128]{4,3,2,1,0:T(8,128)(2,1)S(1)}, bf16[16,8,64,128]{3,2,1,0:T(8,128)(2,1)}, bf16[4,1024,128]{2,1,0:T(8,128)(2,1)S(1)}) custom-call(s32[256]{0:T(256)S(1)} %sub.64.page_ref, s32[32]{0:T(128)S(1)} %copy-done.5, s32[32]{0:T(128)S(1)} %copy-done.6, s32[32]{0:T(128)S(1)} %copy-done.7, ...), custom_call_target="tpu_custom_call" | custom-call | tf_op jit(solution)/shard_map/attend_and_gather/pallas_call | solution.py:209
  69.6 0.3 add_reduce_fusion
  70.2 0.6 select_reduce_fusion.8
  70.9 1.2 select_reduce_fusion.9
  72.0 0.6 reduce_max.9
  73.4 0.2 broadcast_compare_fusion
  73.7 118.4 %conditional.1 = (bf16[2,256,128]{2,1,0:T(8,128)(2,1)S(1)}, bf16[32,128,2,128]{3,2,1,0:T(2,128)(2,1)S(1)}) conditional(s32[]{:T(128)} %clamp.3, (s32[4]{0:T(128)S(1)}, s32[4]{0:T(128)S(1)}, s32[4]{0:T(128)S(1)}, s32[4]{0:T(128)S(1)}, s32[16,128]{1,0:T(8,128)S(1)}, /*index=5*/s32[]{:T(128)}, s32[16,128]{1,0:T(8,128)S(1)}, s32[16,128]{1,0:T(8,128)S(1)}, ...), branch_computations={%region_4.9_spmd, %region_9.14_spmd} | conditional | flops 3148928 | bytes 1395928 | solution.py:477
  73.7 0.6 select_reduce_fusion.2
  74.4 0.1 add_select_fusion
  74.8 0.2 select_reduce_fusion.3.pack_ref
  75.0 117.1 %move_and_project.4 = (bf16[8,4,4,4,16,128]{5,4,3,2,1,0:T(8,128)(2,1)S(1)}, bf16[2,256,128]{2,1,0:T(8,128)(2,1)S(1)}) custom-call(s32[448]{0:T(512)S(1)} %select_reduce_fusion.3.pack_ref, s32[512]{0:T(512)S(1)} %select_n.132.unpack_ref, s32[4,512]{1,0:T(4,128)S(1)} %reshape.327.position_ref, bf16[512,16,128]{2,1,0:T(8,128)(2,1)S(1)} %bitcast.36, ...), custom_call_target="tpu_custom_call" | custom-call | tf_op jit(solution)/shard_map/cond/branch_0_fun/move_and_project/pallas_call | solution.py:394
  192.1 1.3 copy.29
  193.4 0.7 copy.30
  (34 shorter events, 1.0 us)
Async XLA Ops:
  2.3 1.6 copy-start
  3.9 0.9 copy-start.1
  4.9 0.9 copy-start.2
  5.8 0.8 copy-start.3
  6.6 0.8 copy-start.4
  7.4 0.7 copy-start.5
  8.0 0.7 copy-start.6
  8.7 0.7 copy-start.7
  9.3 0.7 copy-start.8

commit v2 on v1

v2 whole, which is shorter than its diff:
```python
import functools
import math

import jax
import jax.numpy as jnp
from jax import lax
from jax.experimental import pallas as pl
from jax.experimental.pallas import tpu as pltpu
from jax.sharding import PartitionSpec as P

MESH = pl.DeviceIdType.MESH
BF16, F32, I32 = jnp.bfloat16, jnp.float32, jnp.int32
HEAD = 128
X, Z, T = 4, 16, 8
S = 32
UNITS = 16
LANE_UNITS = UNITS // X
CAPACITIES = ((24, 64), (26, 64), (28, 72), (30, 72), (34, 80), (64, 128))
QUARTER = 8
masked_score = -1e30

VM = pl.BlockSpec(memory_space=pltpu.VMEM)
SM = pl.BlockSpec(memory_space=pltpu.SMEM)
HB = pl.BlockSpec(memory_space=pltpu.HBM)


def place():
    r = lax.axis_index("replica")
    return r // X, lax.rem(r, X), lax.axis_index("tensor")


def to_replica(z, x):
    return dict(device_id={"replica": z * X + x}, device_id_type=MESH)


def to_tensor(t):
    return dict(device_id={"tensor": t}, device_id_type=MESH)


def attend_kernel(
    facts_ref, own_facts_ref, pool_hbm, query_hbm, fresh_hbm, prompt_hbm,
    all_facts_ref, xbuf_ref, gathered_ref, position_ref, table_ref,
    pool_ref, query_ref, fresh_ref, prompt_ref, cache, split, heads, fresh32, by_plane, offsets, found,
    in_sem, f_send, f_recv, g_send, g_recv, x_send, x_recv, r_send, r_recv, l_send, l_recv, own_sem,
):
    z, x, _ = place()
    up, down = lax.rem(z + 1, Z), lax.rem(z + Z - 1, Z)
    barrier = pltpu.get_barrier_semaphore()
    inputs = [
        pltpu.make_async_copy(a, b, in_sem.at[i])
        for i, (a, b) in enumerate(
            ((fresh_hbm, fresh_ref), (pool_hbm, pool_ref), (query_hbm, query_ref), (prompt_hbm, prompt_ref))
        )
    ]
    for copy in inputs:
        copy.start()
    for i in range(1, X):
        pl.semaphore_signal(barrier, inc=1, **to_replica(z, lax.rem(x + i, X)))

    @pl.loop(1, Z)
    def _(i):
        pl.semaphore_signal(barrier, inc=1, **to_replica(lax.rem(z + i, Z), x))

    page_of = lambda s, i: facts_ref[s * 8 + i]
    slot_of = lambda s: facts_ref[256 + s]
    length_of = lambda s: facts_ref[288 + s]
    group_of = lambda s: facts_ref[320 + s]
    prompt_length_of = lambda group: facts_ref[352 + group]

    mine = all_facts_ref.at[z, pl.ds(x, 1)]
    all_facts_ref[z, pl.ds(x, 1)] = own_facts_ref[...]

    def f_copy(i):
        return pltpu.make_async_remote_copy(
            mine, mine, f_send.at[i], f_recv.at[i], **to_replica(z, lax.rem(x + i, X))
        )

    def g_copy(i):
        return pltpu.make_async_remote_copy(
            all_facts_ref.at[z], all_facts_ref.at[z], g_send.at[i], g_recv.at[i], **to_replica(lax.rem(z + i, Z), x)
        )

    def x_copy(i, quarter):
        lane = lax.rem(x + i, X)
        rows = pl.ds(quarter * QUARTER, QUARTER)
        return pltpu.make_async_remote_copy(
            split.at[lane, rows], xbuf_ref.at[x, rows], x_send.at[i, quarter], x_recv.at[i, quarter],
            **to_replica(z, lane),
        )

    row = lax.broadcasted_iota(I32, (16, HEAD), 0)
    odd = lax.rem(row, 2) == 1
    token_of_row = row // 2

    def build(s):
        length = length_of(s)
        one = jnp.where(odd, fresh32[pl.ds(4 * s + 1, 1), :], fresh32[pl.ds(4 * s, 1), :])
        two = jnp.where(odd, fresh32[pl.ds(4 * s + 3, 1), :], fresh32[pl.ds(4 * s + 2, 1), :])
        for page in range(8):
            source = page_of(s, page)
            for half in range(2):
                unit = pool_ref[source, 16 * half : 16 * (half + 1), :].astype(F32)
                token = token_of_row + (16 * page + 8 * half) - length
                unit = jnp.where(
                    token < 0, unit, jnp.where(token == 0, one, jnp.where(token == 1, two, 0.0))
                )
                cache[s, 2 * page + half] = unit.astype(BF16)

    def divide(s):
        slot = slot_of(s)
        for lane in range(X):
            turn = lax.rem(lane + 4 * S - lax.rem(slot, 4), 4)
            for k in range(LANE_UNITS):
                split[lane, s, k] = cache[s, 4 * k + turn]

    scale = 1.0 / math.sqrt(HEAD)
    column = lax.broadcasted_iota(I32, (16, 256), 1)
    step = lax.rem(lax.broadcasted_iota(I32, (16, 256), 0), 2)
    suffix_token = column // 2 - 1 - step
    is_key = lax.rem(column, 2) == 0
    pcolumn = lax.broadcasted_iota(I32, (16, HEAD), 1)
    is_pkey = lax.rem(pcolumn, 2) == 0
    by_column = (((1,), (1,)), ((), ()))

    def attend(s):
        query = query_ref[s]
        group = lax.rem(group_of(s), 2)
        prompt = prompt_ref[group]
        entries = cache[s].reshape(256, HEAD)
        seen = is_key & (suffix_token < length_of(s))
        pseen = is_pkey & (pcolumn // 2 < prompt_length_of(group))
        scores = lax.dot_general(query, entries, by_column, preferred_element_type=F32) * scale
        pscores = lax.dot_general(query, prompt, by_column, preferred_element_type=F32) * scale
        scores = jnp.where(seen, scores, masked_score)
        pscores = jnp.where(pseen, pscores, masked_score)
        top = jnp.maximum(
            jnp.max(scores, axis=1, keepdims=True), jnp.max(pscores, axis=1, keepdims=True)
        )
        weights = jnp.where(seen, jnp.exp(scores - top), 0.0)
        pweights = jnp.where(pseen, jnp.exp(pscores - top), 0.0)
        total = jnp.sum(weights, axis=1, keepdims=True) + jnp.sum(pweights, axis=1, keepdims=True)
        weights = pltpu.roll(weights, 1, 1).astype(BF16)
        pweights = pltpu.roll(pweights, 1, 1).astype(BF16)
        out = jnp.dot(weights, entries, preferred_element_type=F32)
        out = out + jnp.dot(pweights, prompt, preferred_element_type=F32)
        return out / total

    def ring(step, part, forward):
        plane = lax.rem(z + Z - step, Z) if forward else lax.rem(z + step, Z)
        block = gathered_ref.at[plane, part]
        send, recv = (r_send, r_recv) if forward else (l_send, l_recv)
        return pltpu.make_async_remote_copy(
            block, block, send.at[2 * step + part], recv.at[2 * step + part],
            **to_replica(up if forward else down, x),
        )

    for copy in inputs[:2]:
        copy.wait()
    fresh32[...] = fresh_ref[...].astype(F32)
    for quarter in range(S // QUARTER):

        @pl.loop(0, QUARTER)
        def _(n):
            build(quarter * QUARTER + n)

        @pl.loop(0, QUARTER)
        def _(n):
            divide(quarter * QUARTER + n)

        if quarter == 0:
            pl.semaphore_wait(barrier, X + Z - 2)
            for i in range(1, X):
                f_copy(i).start()
            for copy in inputs[2:]:
                copy.wait()
        for i in range(1, X):
            x_copy(i, quarter).start()

        @pl.loop(0, QUARTER // 4)
        def _(block):
            first = quarter * QUARTER + 4 * block
            outs = [attend(first + i) for i in range(4)]
            for i, out in enumerate(outs):
                for head in range(8):
                    for k in range(2):
                        place_in = (quarter % 2) * QUARTER + 4 * block + i + k * (S // 2)
                        heads[head, pl.ds(place_in, 1), :] = out[2 * head + k : 2 * head + k + 1]

        if quarter % 2:
            part = quarter // 2
            gathered_ref[z, part] = heads[...].astype(BF16)
            ring(0, part, True).start()
            ring(0, part, False).start()
        if quarter == 1:
            for i in range(1, X):
                f_copy(i).wait()

            @pl.loop(1, Z)
            def _(i):
                g_copy(i).start()

    own_split = pltpu.make_async_copy(split.at[x], xbuf_ref.at[x], own_sem.at[0])
    own_split.start()

    def iota(rows, axis):
        return lax.broadcasted_iota(I32, (rows, HEAD), axis)

    def units_on(lane, slot, filled):
        return (filled - ((lane - slot) & 3) + 3) >> 2

    def pick(a, b):
        return lax.dot_general(a.astype(F32).astype(BF16), b.astype(F32).astype(BF16), by_column, preferred_element_type=F32)

    def gather_facts():
        @pl.loop(1, Z)
        def _(i):
            g_copy(i).wait()

        part = lambda plane, lane: all_facts_ref[plane, lane][:, :S]
        for plane in range(Z):
            by_plane[plane : plane + 1, :] = jnp.concatenate([part(plane, lane) for lane in range(X)], axis=1)
        for lane in range(X):
            row = jnp.concatenate([part(plane, lane) for plane in range(Z)], axis=1)
            position_ref[lane : lane + 1, :] = row >> 7

    def decode(facts):
        return facts >> 7, ((facts & 127) + 9) >> 3

    def pairs():
        position, filled = decode(by_plane[...])
        count = [units_on(lane, position, filled) for lane in range(X)]
        return position, [(count[0] + (count[1] << 12)).astype(F32), (count[2] + (count[3] << 12)).astype(F32)]

    def larger(most, total):
        total = total.astype(I32)
        return jnp.maximum(most, jnp.maximum(total & 4095, total >> 12))

    def find_offsets():
        position, filled = decode(by_plane[...])
        plane = position >> 7
        count = units_on(x, position, filled).astype(F32)
        groups = [plane == i for i in range(Z)]
        stacked = jnp.concatenate([jnp.where(g, count, 0.0) for g in groups], axis=0)
        earlier = (iota(HEAD, 1) < iota(HEAD, 0)).astype(F32)
        sums = pick(stacked, earlier)
        offset = jnp.zeros((Z, HEAD), F32)
        for i, g in enumerate(groups):
            offset = offset + jnp.where(g, sums[i * Z : (i + 1) * Z], 0.0)
        offsets[...] = offset
        mine = iota(Z, 0) == z
        own = lambda a: jnp.sum(jnp.where(mine, a, 0.0), axis=0, keepdims=True)
        own_count, own_offset = own(count), own(offset)
        target = (own(plane.astype(F32)).astype(I32) == iota(Z, 0)).astype(F32)
        ahead = iota(HEAD, 0).astype(F32) - own_offset
        here = ((ahead >= 0.0) & (ahead < own_count)).astype(F32)
        sibling = pick(target * iota(Z, 1).astype(F32), here)
        unit = pick(target, here * ahead)
        table_ref[0:Z, :] = (4.0 * sibling + unit).astype(I32)

    def find_sources():
        wanted = iota(HEAD, 0) + z * (X * S)
        row = iota(8, 0)
        total = jnp.zeros((8, HEAD), F32)
        for plane in range(Z):
            position, filled = decode(by_plane[plane : plane + 1, :])
            values = jnp.where(row == 0, float(plane), jnp.where(row == 1, offsets[plane : plane + 1, :], filled.astype(F32)))
            total = total + pick(values, (position == wanted).astype(F32))
        found[...] = total

    def find_deliveries():
        plane, offset, filled = found[0:1, :], found[1:2, :], found[2:3, :].astype(I32)
        slot, row = iota(1, 1) & (S - 1), iota(8, 0)
        comes = [units_on(lane, slot, filled).astype(F32) for lane in range(X)]
        leaves = units_on(x, slot, filled).astype(F32)
        stacked = jnp.broadcast_to(leaves, (8, HEAD))
        for lane in range(X):
            stacked = jnp.where(row == lane, comes[lane], stacked)
        near = (iota(HEAD, 1) < iota(HEAD, 0)) & ((iota(HEAD, 1) >> 5) == (iota(HEAD, 0) >> 5))
        sums = pick(stacked, near.astype(F32))
        ahead = iota(HEAD, 0).astype(F32) - sums[4:5]
        here = ((ahead >= 0.0) & (ahead < leaves)).astype(F32)
        target = ((iota(8, 1) >> 5) == row).astype(F32)
        spot = 64.0 * pick(target * plane, here) + pick(target * (offset - sums[4:5]), here)
        table_ref[16:24, :] = (spot + pick(target, here) * iota(8, 1).astype(F32)).astype(I32)
        for j in range(X):
            lane = (slot + j) & 3
            first, count = jnp.zeros((1, HEAD), F32), jnp.zeros((1, HEAD), F32)
            for i in range(X):
                first = first + jnp.where(lane == i, sums[i : i + 1] + 128.0 * i, 0.0)
                count = count + jnp.where(lane == i, comes[i], 0.0)
            for k in range(LANE_UNITS):
                value = jnp.where(count > float(k), first + float(k), 128.0 * X)
                table_ref[24 + 4 * k + j : 25 + 4 * k + j, :] = value.astype(I32)

    def find_largest():
        position, counts = pairs()
        largest = jnp.zeros((Z, 1), I32)
        for plane in range(Z):
            for count in counts:
                largest = larger(largest, jnp.sum(jnp.where((position >> 7) == plane, count, 0.0), axis=1, keepdims=True))
        largest = jnp.max(largest.astype(F32), axis=0, keepdims=True).astype(I32)
        table_ref[40:41, :] = jnp.broadcast_to(largest, (1, HEAD))

    def find_most():
        position, counts = pairs()

        def one(replica, most):
            here = (position >> 5) == replica
            for count in counts:
                total = jnp.sum(jnp.sum(jnp.where(here, count, 0.0), axis=0, keepdims=True), axis=1, keepdims=True)
                most = larger(most, total)
            return most

        most = lax.fori_loop(0, Z * X, one, jnp.zeros((1, 1), I32))
        largest = table_ref[40:41, :]
        choice = jnp.zeros((1, HEAD), I32)
        for units, delivered in CAPACITIES[:-1]:
            choice = choice + ((largest > units) | (most > delivered)).astype(I32)
        table_ref[41:48, :] = jnp.broadcast_to(choice, (7, HEAD))

    between = [None, gather_facts, find_offsets, find_sources, find_deliveries, find_largest, find_most, None]

    for step in range(1, Z // 2):
        for part in range(2):
            for forward in (True, False):
                if not forward and step == Z // 2 - 1:
                    continue
                ring(step - 1, part, forward).wait_recv()
                ring(step, part, forward).start()
        if between[step]:
            between[step]()
    for part in range(2):
        ring(Z // 2 - 1, part, True).wait_recv()
        ring(Z // 2 - 2, part, False).wait_recv()
    for step in range(Z // 2):
        for part in range(2):
            for forward in (True, False):
                if not forward and step == Z // 2 - 1:
                    continue
                ring(step, part, forward).wait_send()

    for i in range(1, X):
        for quarter in range(S // QUARTER):
            x_copy(i, quarter).wait()
    own_split.wait()


def attend_call(facts, own_facts, pool, query, fresh, prompt):
    dma = pltpu.SemaphoreType.DMA
    return pl.pallas_call(
        attend_kernel,
        out_shape=(
            jax.ShapeDtypeStruct((Z, X, 1, HEAD), I32),
            jax.ShapeDtypeStruct((X, S, LANE_UNITS, 16, HEAD), BF16),
            jax.ShapeDtypeStruct((Z, 2, 8, S, HEAD), BF16),
            jax.ShapeDtypeStruct((X, Z * S), I32),
            jax.ShapeDtypeStruct((48, HEAD), I32),
        ),
        in_specs=[SM, VM] + [HB] * 4,
        out_specs=(VM,) * 5,
        scratch_shapes=[
            pltpu.VMEM(pool.shape, BF16),
            pltpu.VMEM(query.shape, BF16),
            pltpu.VMEM(fresh.shape, BF16),
            pltpu.VMEM(prompt.shape, BF16),
            pltpu.VMEM((S, UNITS, 16, HEAD), BF16),
            pltpu.VMEM((X, S, LANE_UNITS, 16, HEAD), BF16),
            pltpu.VMEM((8, S, HEAD), F32),
            pltpu.VMEM((4 * S, HEAD), F32),
            pltpu.VMEM((Z, HEAD), I32),
            pltpu.VMEM((Z, HEAD), F32),
            pltpu.VMEM((8, HEAD), F32),
            dma((4,)), dma((X,)), dma((X,)), dma((Z,)), dma((Z,)), dma((X, 4)), dma((X, 4)),
            dma((Z,)), dma((Z,)), dma((Z,)), dma((Z,)), dma((1,)),
        ],
        compiler_params=pltpu.CompilerParams(
            collective_id=1, has_side_effects=True, vmem_limit_bytes=60 << 20
        ),
        name="attend_and_gather",
    )(facts, own_facts, pool, query, fresh, prompt)


def move_kernel(
    capacity, delivery,
    table_ref, position_ref, xbuf_ref, gathered_ref, weight_ref,
    moved_ref, block_ref,
    packed, arrived, wide, product, columns, chunk, chunks, outgoing, incoming,
    z_send, z_recv, w_send, w_recv, c_send, c_recv, t_send, t_recv, d_send, d_recv, own_sem,
):
    z, x, t = place()
    barrier = pltpu.get_barrier_semaphore()

    @pl.loop(1, Z)
    def _(i):
        pl.semaphore_signal(barrier, inc=1, **to_replica(lax.rem(z + i, Z), x))

    for i in range(1, X):
        pl.semaphore_signal(barrier, inc=1, **to_replica(z, lax.rem(x + i, X)))
    for i in range(1, T):
        pl.semaphore_signal(barrier, inc=1, **to_tensor(lax.rem(t + i, T)))
    pl.semaphore_wait(barrier, Z + X + T - 3)

    def z_copy(i):
        plane = lax.rem(z + i, Z)
        return pltpu.make_async_remote_copy(
            packed.at[plane], arrived.at[z], z_send.at[i], z_recv.at[i], **to_replica(plane, x)
        )

    @pl.loop(0, Z)
    def _(i):
        plane = lax.rem(z + i, Z)
        for c in range(capacity):
            packed[plane, c] = xbuf_ref[table_ref[plane, c]]

        @pl.when(i > 0)
        def _():
            z_copy(i).start()

    own_plane = pltpu.make_async_copy(packed.at[z], arrived.at[z], own_sem.at[0])
    own_plane.start()
    incoming[X, 0] = jnp.zeros((16, HEAD), BF16)

    def w_copy(i):
        return pltpu.make_async_remote_copy(
            weight_ref, wide.at[x], w_send.at[i], w_recv.at[i], **to_replica(z, lax.rem(x + i, X))
        )

    for i in range(1, X):
        w_copy(i).start()
    own_weight = pltpu.make_async_copy(weight_ref, wide.at[x], own_sem.at[3])
    own_weight.start()
    own_weight.wait()
    for i in range(1, X):
        w_copy(i).wait()

    @pl.loop(0, Z // 4)
    def _(b):
        blocks = gathered_ref[pl.ds(4 * b, 4)]
        rows = jnp.concatenate([blocks[:, :, h].reshape(8 * S, HEAD) for h in range(8)], axis=1)
        for pair in range(X // 2):
            weight = jnp.concatenate([wide[2 * pair], wide[2 * pair + 1]], axis=1)
            out = jnp.dot(rows, weight, preferred_element_type=F32).astype(BF16)
            out = out.reshape(4, 2, 2, S // 2, 2 * HEAD)
            for i in range(2):
                for k in range(2):
                    part = out[:, :, k, :, i * HEAD : (i + 1) * HEAD].reshape(4 * S, HEAD)
                    product[2 * pair + i, k, pl.ds(pl.multiple_of(b * 4 * S, 4 * S), 4 * S), :] = part

    def c_copy(i):
        lane = lax.rem(x + i, X)
        return pltpu.make_async_remote_copy(
            product.at[lane], columns.at[x], c_send.at[i], c_recv.at[i], **to_replica(z, lane)
        )

    for i in range(1, X):
        c_copy(i).start()
    own_columns = pltpu.make_async_copy(product.at[x], columns.at[x], own_sem.at[1])
    own_columns.start()
    own_columns.wait()
    for i in range(1, X):
        c_copy(i).wait()

    def t_copy(i):
        other = lax.rem(t + i, T)
        return pltpu.make_async_remote_copy(
            chunk.at[other], chunks.at[t], t_send.at[i], t_recv.at[i], **to_tensor(other)
        )

    @pl.loop(0, T)
    def _(n):
        i = lax.rem(n + 1, T)
        other = lax.rem(t + i, T)
        target = lax.broadcasted_iota(I32, (8 * S, Z * S), 0) + other * (8 * S)
        total = jnp.zeros((8 * S, 2 * HEAD), F32)
        for lane in range(X):
            pick = (position_ref[pl.ds(lane, 1), :] == target).astype(F32).astype(BF16)
            rows = jnp.concatenate([columns[lane, 0], columns[lane, 1]], axis=1)
            total = total + jnp.dot(pick, rows, preferred_element_type=F32)
        for k in range(2):
            chunk[other, k] = total[:, k * HEAD : (k + 1) * HEAD].astype(BF16)

        @pl.when(i > 0)
        def _():
            t_copy(i).start()

    own_chunk = pltpu.make_async_copy(chunk.at[t], chunks.at[t], own_sem.at[2])
    own_chunk.start()
    own_chunk.wait()
    for i in range(1, T):
        t_copy(i).wait()
    for k in range(2):
        total = chunks[0, k].astype(F32)
        for n in range(1, T):
            total = total + chunks[n, k].astype(F32)
        block_ref[k] = total.astype(BF16)

    own_plane.wait()

    @pl.loop(1, Z)
    def _(i):
        z_copy(i).wait()

    def d_copy(i):
        lane = lax.rem(x + i, X)
        return pltpu.make_async_remote_copy(
            outgoing.at[lane], incoming.at[x, pl.ds(0, delivery)], d_send.at[i], d_recv.at[i], **to_replica(z, lane)
        )

    @pl.loop(0, X)
    def _(n):
        i = lax.rem(n + 1, X)
        lane = lax.rem(x + i, X)

        @pl.loop(0, delivery // 8)
        def _(c):
            for j in range(8):
                index = table_ref[16 + lane, 8 * c + j]
                outgoing[lane, 8 * c + j] = arrived[index // 64, lax.rem(index, 64)]

        @pl.when(i > 0)
        def _():
            d_copy(i).start()

    own_delivery = pltpu.make_async_copy(outgoing.at[x], incoming.at[x, pl.ds(0, delivery)], own_sem.at[4])
    own_delivery.start()
    own_delivery.wait()
    for i in range(1, X):
        d_copy(i).wait()

    @pl.loop(0, S)
    def _(slot):
        for unit in range(UNITS):
            index = table_ref[24 + unit, x * S + slot]
            moved_ref[slot // 4, lax.rem(slot, 4), unit // 4, unit % 4] = incoming[index // 128, lax.rem(index, 128)]


def move_call(number, capacity, delivery, *operands):
    dma = pltpu.SemaphoreType.DMA
    return pl.pallas_call(
        functools.partial(move_kernel, capacity, delivery),
        out_shape=(
            jax.ShapeDtypeStruct((S // 4, 4, UNITS // 4, 4, 16, HEAD), BF16),
            jax.ShapeDtypeStruct((2, 8 * S, HEAD), BF16),
        ),
        in_specs=[SM, VM, VM, VM, HB],
        out_specs=(VM, VM),
        scratch_shapes=[
            pltpu.VMEM((Z, capacity, 16, HEAD), BF16),
            pltpu.VMEM((Z, capacity, 16, HEAD), BF16),
            pltpu.VMEM((X, 8 * HEAD, HEAD), BF16),
            pltpu.VMEM((X, 2, Z * S, HEAD), BF16),
            pltpu.VMEM((X, 2, Z * S, HEAD), BF16),
            pltpu.VMEM((T, 2, 8 * S, HEAD), BF16),
            pltpu.VMEM((T, 2, 8 * S, HEAD), BF16),
            pltpu.VMEM((X, delivery, 16, HEAD), BF16),
            pltpu.VMEM((X + 1, delivery, 16, HEAD), BF16),
            dma((Z,)), dma((Z,)), dma((X,)), dma((X,)), dma((X,)), dma((X,)), dma((T,)), dma((T,)),
            dma((X,)), dma((X,)), dma((5,)),
        ],
        compiler_params=pltpu.CompilerParams(
            collective_id=2 + number, has_side_effects=True, vmem_limit_bytes=48 << 20
        ),
        name="move_and_project",
    )(*operands)


def body(
    queries, fresh_entries, suffix_page_pool, page_table, suffix_len,
    prompt_key_value, prompt_len, sibling_group, new_position, output_weight,
):
    z, x, _ = place()
    numbers = jnp.concatenate(
        [page_table.reshape(-1) - (z * X + x) * (S * 8), new_position, suffix_len, sibling_group, prompt_len,
         jnp.zeros((30,), I32)]
    )
    own_facts = jnp.pad(new_position * 128 + suffix_len, (0, HEAD - S)).reshape(1, 1, HEAD)
    query = queries.reshape(S, 2, 8, HEAD).transpose(0, 2, 1, 3).reshape(S, 16, HEAD)
    _, xbuf, gathered, position, table = attend_call(
        numbers, own_facts, suffix_page_pool.reshape(S * 8, 32, HEAD), query,
        fresh_entries.reshape(4 * S, HEAD), prompt_key_value.reshape(2, 2 * 64, HEAD),
    )
    moved, block = lax.switch(
        table[41, 0], [functools.partial(move_call, n, c, d) for n, (c, d) in enumerate(CAPACITIES)],
        table, position, xbuf.reshape(X * S * LANE_UNITS, 16, HEAD), gathered, output_weight,
    )
    return moved.reshape(S, 128, 2, HEAD), block


def solution(mesh):
    placed = (
        P("replica", None, "tensor"),
        P("replica", None, None, "tensor"),
        P("replica", None, None, "tensor"),
        P("replica", None),
        P("replica"),
        P("replica", None, None, "tensor"),
        P("replica"),
        P("replica"),
        P("replica"),
        P("tensor", "replica"),
    )
    return jax.shard_map(
        body,
        mesh=mesh,
        in_specs=placed,
        out_specs=(P("replica", None, None, "tensor"), P(None, "tensor", "replica")),
        check_vma=False,
    )
```

time: 196 us -> 170 us (0.87); the launches traced: 194 us -> 170 us
  Pallas kernels: 177 us -> 163 us
  local copies, waits for them, and re-layouts: 10.5 us -> 4.55 us
  other arithmetic: 5.45 us -> 1.41 us
    pallas_call x1, Pallas kernels: 117 us -> 103 us  [move_call(): pl.pallas_call(functools.partial(move_kernel, capacity, delivery), out_sh...]
    unnamed x20 -> x4, local copies, waits for them, and re-layouts: 9.63 us -> 1.98 us
    reduce_sum x5 -> x0, other arithmetic: 2.63 us -> none  [the longest x1 1.15 us: body(): jnp.sum(jnp.where(plane[None, :, None, :] == planes[None, None, :, None],...]
where the time goes in v2:
time: 170 us
  Pallas kernels  163 us (96%)
  local copies, waits for them, and re-layouts  4.55 us (3%)
    pallas_call x1, Pallas kernels, move_call(): pl.pallas_call(functools.partial(move_kernel, capacity, delivery), out_sh...  103 us
    pallas_call x1, Pallas kernels, attend_call(): pl.pallas_call(attend_kernel, out_shape=(jax.ShapeDtypeStruct((Z, X, 1, H...  59.6 us

profile of v2, /device:TPU:1, one launch (start us, length us, event | category | flops | bytes accessed | tf_op | source)
XLA Modules:
  0.0 170.1 jit_solution(7149236573508007566)
XLA Ops:
  0.6 0.0 copy-start
  0.7 0.7 multiply_add_fusion
  1.4 0.5 pad_bitcast_fusion.own_facts_ref
  1.9 0.7 broadcast_subtract_fusion
  2.6 0.1 copy.13
  2.7 0.1 sub.16
  2.8 1.4 concatenate.3.facts_ref
  4.1 59.6 %attend_and_gather.1 = (s32[16,4,1,128]{3,2,1,0:T(1,128)}, bf16[4,32,4,16,128]{4,3,2,1,0:T(8,128)(2,1)S(1)}, bf16[16,2,8,32,128]{4,3,2,1,0:T(8,128)(2,1)}, s32[4,512]{1,0:T(4,128)S(1)}, s32[48,128]{1,0:T(8,128)S(1)}) custom-call(s32[384]{0:T(512)} %concatenate.3.facts_ref, s32[1,1,128]{2,1,0:T(1,128)} %pad_bitcast_fusion.own_facts_ref, ...), custom_call_target="tpu_custom_call" | custom-call | tf_op jit(solution)/shard_map/attend_and_gather/pallas_call | solution.py:350
  63.7 0.5 slice.3
  64.9 0.0 copy-done
  64.9 103.3 %conditional.1 = (bf16[2,256,128]{2,1,0:T(8,128)(2,1)S(1)}, bf16[32,128,2,128]{3,2,1,0:T(2,128)(2,1)S(1)}) conditional(s32[]{:T(128)} %bitcast.13, (s32[48,128]{1,0:T(8,128)S(1)}, s32[4,512]{1,0:T(4,128)S(1)}, bf16[512,16,128]{2,1,0:T(8,128)(2,1)S(1)}, bf16[16,2,8,32,128]{4,3,2,1,0:T(8,128)(2,1)}, ...), branch_computations={%region_0.1_spmd, %region_1.2_spmd, %region_2.3_spmd, %region_3.4_... | conditional | bytes 16 | solution.py:582
  64.9 103.2 %move_and_project.6 = (bf16[8,4,4,4,16,128]{5,4,3,2,1,0:T(8,128)(2,1)S(1)}, bf16[2,256,128]{2,1,0:T(8,128)(2,1)S(1)}) custom-call(s32[48,128]{1,0:T(8,128)S(1)} %get-tuple-element.73.table_ref, s32[4,512]{1,0:T(4,128)S(1)} %get-tuple-element.74.position_ref, bf16[512,16,128]{2,1,0:T(8,128)(2,1)S(1)} %get-tuple-element.75.xbuf_ref, ...), custom_call_target="tpu_custom_call" | custom-call | tf_op jit(solution)/shard_map/cond/branch_0_fun/move_and_project/pallas_call | solution.py:539
  168.2 1.3 copy.29
  169.5 0.7 copy.30
  (1 shorter events, 0.0 us)
Async XLA Ops:
  0.6 64.3 %copy-start = (bf16[1024,128]{1,0:T(8,128)(2,1)S(1)}, bf16[1024,128]{1,0:T(8,128)(2,1)}, u32[]{:S(2)}) copy-start(bf16[1024,128]{1,0:T(8,128)(2,1)} %param.25) | copy-start | bytes 786436
